TPU v7x, 32 devices: a whole 2x2x4 slice. The times are simulated.
32 devices in a mesh: copy: 4 (over x, core), space: 8 (over z, y).
Axes of the slice: x: 2, y: 2, z: 4, core: 2. Of those that a mesh axis runs over, the one named last changes fastest.
Arguments:
- noisy_tokens: bfloat16 [4, 256, 256, 384], P('copy', 'space'), may hold values from -6 to 6
- grad_out: bfloat16 [4, 256, 256, 384], P('copy', 'space'), may hold values from -6 to 6
- filter_weight: bfloat16 [2, 256, 256, 384], P(None, None, 'space'), may hold values from -4 to 4
- weight_in: bfloat16 [384, 1536], replicated, may hold values from -0.3125 to 0.3125
- weight_out: bfloat16 [1536, 384], replicated, may hold values from -0.15625 to 0.15625
- gain_one: float32 [384], replicated, may hold values from 0.1 to 1.9
- gain_two: float32 [384], replicated, may hold values from 0.1 to 1.9
Outputs:
- block_out: bfloat16 [4, 256, 256, 384], P('copy', 'space')
- grad_tokens: bfloat16 [4, 256, 256, 384], P('copy', 'space')
- grad_filter: float32 [2, 256, 256, 384], P(None, None, 'space')
- grad_weight_in: bfloat16 [384, 1536], replicated
- grad_weight_out: bfloat16 [1536, 384], replicated
- grad_gain_one: float32 [384], replicated
- grad_gain_two: float32 [384], replicated
All inputs are finite; a program needn't handle non-finite values.
Results may differ from a plain program's by a relative error of at most 0.024.
Values may be sent and summed in bfloat16 or wider, within the bound.
No kernel may reach another device: no remote copies, remote signals or barrier semaphores. Data moves between devices by JAX's collectives and lax.ppermute only.
A program may use at most 320 MiB of HBM per device.

v0:
```python
import math

import jax
import jax.numpy as jnp
from jax import lax
from jax.sharding import PartitionSpec as P

EPS = 1e-06


def dft_parts(length):
    index = jnp.arange(length, dtype=jnp.int32)
    phase = index[:, None] * index[None, :] % length
    angle = phase.astype(jnp.float32) * (2.0 * math.pi / length)
    factor = 1.0 / math.sqrt(length)
    return (
        (jnp.cos(angle) * factor).astype(jnp.bfloat16),
        (jnp.sin(angle) * factor).astype(jnp.bfloat16),
    )


def row_table(length):
    cosine, sine = dft_parts(length)
    return jnp.stack([cosine, -sine])


def column_table(length, direction):
    cosine, sine = dft_parts(length)
    upper = jnp.stack([cosine, direction * sine], axis=1)
    lower = jnp.stack([-direction * sine, cosine], axis=1)
    return jnp.stack([upper, lower])


def layer_norm(values):
    centre = jnp.mean(values, axis=-1, keepdims=True)
    centred = values - centre
    variance = jnp.mean(centred * centred, axis=-1, keepdims=True)
    rstd_value = lax.rsqrt(variance + EPS)
    return (centred * rstd_value, rstd_value)


def norm_backward(upstream, normed, rstd_value, gain):
    scaled = upstream * gain
    result = (
        scaled
        - jnp.mean(scaled, axis=-1, keepdims=True)
        - normed * jnp.mean(scaled * normed, axis=-1, keepdims=True)
    ) * rstd_value
    lead = tuple(range(upstream.ndim - 1))
    return (result, jnp.sum(upstream * normed, axis=lead))


def apply_filter(spectrum, filter_weight, direction):
    real_part = spectrum[0].astype(jnp.float32)
    imag_part = spectrum[1].astype(jnp.float32)
    kernel_real = filter_weight[0].astype(jnp.float32)
    kernel_imag = direction * filter_weight[1].astype(jnp.float32)
    return jnp.stack(
        [
            kernel_real * real_part - kernel_imag * imag_part,
            kernel_real * imag_part + kernel_imag * real_part,
        ]
    )


def exact_gelu(values):
    return jax.nn.gelu(values, approximate=False)


def spectral(values, filter_weight, direction):
    width = values.shape[2]
    rows_tab = row_table(width)
    rows = jnp.einsum(
        "pkw,bhwc->pbhkc", rows_tab, values, preferred_element_type=jnp.float32
    ).astype(jnp.bfloat16)
    columns = lax.all_to_all(rows, "space", split_axis=3, concat_axis=2, tiled=True)
    height = columns.shape[2]
    spectrum = jnp.einsum(
        "qmph,pbhkc->qbmkc", column_table(height, 1), columns, preferred_element_type=jnp.float32
    ).astype(jnp.bfloat16)
    weighted = apply_filter(spectrum, filter_weight[:, None], direction).astype(jnp.bfloat16)
    returned = jnp.einsum(
        "qmph,pbhkc->qbmkc", column_table(height, -1), weighted, preferred_element_type=jnp.float32
    ).astype(jnp.bfloat16)
    back_rows = lax.all_to_all(returned, "space", split_axis=2, concat_axis=3, tiled=True)
    output = jnp.einsum("pkw,pbhkc->bhwc", rows_tab, back_rows, preferred_element_type=jnp.float32)
    return (output, spectrum)


def body(noisy_tokens, grad_out, filter_weight, weight_in, weight_out, gain_one, gain_two):
    batch, rows_dev, width, chans = noisy_tokens.shape
    inputs = noisy_tokens.astype(jnp.float32)
    normed_one, rstd_one = layer_norm(inputs)
    mixed_in = (normed_one * gain_one).astype(jnp.bfloat16)
    spatial, spectrum = spectral(mixed_in, filter_weight, 1)
    normed_two, rstd_two = layer_norm(spatial)
    mlp_in = (normed_two * gain_two).astype(jnp.bfloat16).reshape(-1, chans)
    preact = jnp.dot(mlp_in, weight_in, preferred_element_type=jnp.float32)
    activated = exact_gelu(preact).astype(jnp.bfloat16)
    mlp_out = jnp.dot(activated, weight_out, preferred_element_type=jnp.float32)
    block_out = (inputs + mlp_out.reshape(inputs.shape)).astype(jnp.bfloat16)
    upstream = grad_out.reshape(-1, chans)
    grad_act = jnp.dot(upstream, weight_out.T, preferred_element_type=jnp.float32)
    grad_pre = jax.vjp(exact_gelu, preact)[1](grad_act)[0].astype(jnp.bfloat16)
    sum_out = jnp.dot(activated.T, upstream, preferred_element_type=jnp.float32)
    sum_in = jnp.dot(mlp_in.T, grad_pre, preferred_element_type=jnp.float32)
    grad_mlp = jnp.dot(grad_pre, weight_in.T, preferred_element_type=jnp.float32).reshape(
        inputs.shape
    )
    grad_spatial, sum_gain_two = norm_backward(grad_mlp, normed_two, rstd_two, gain_two)
    back_spatial, adjoint = spectral(grad_spatial.astype(jnp.bfloat16), filter_weight, -1)
    spec_f = spectrum.astype(jnp.float32)
    adj_f = adjoint.astype(jnp.float32)
    filter_terms = jnp.stack(
        [
            jnp.sum(adj_f[0] * spec_f[0] + adj_f[1] * spec_f[1], axis=0),
            jnp.sum(adj_f[1] * spec_f[0] - adj_f[0] * spec_f[1], axis=0),
        ]
    )
    grad_filter = lax.psum(filter_terms.astype(jnp.bfloat16), "copy").astype(jnp.float32)
    grad_normed, sum_gain_one = norm_backward(back_spatial, normed_one, rstd_one, gain_one)
    grad_tokens = (grad_out.astype(jnp.float32) + grad_normed).astype(jnp.bfloat16)
    local_sums = (sum_in, sum_out, sum_gain_one, sum_gain_two)
    summed = lax.psum(
        (local_sums[0], local_sums[1], local_sums[2], local_sums[3]), ("copy", "space")
    )
    total_tokens = batch * lax.axis_size("copy") * rows_dev * lax.axis_size("space") * width
    factor = 1.0 / math.sqrt(total_tokens)
    return (
        block_out,
        grad_tokens,
        grad_filter,
        (summed[0] * factor).astype(jnp.bfloat16),
        (summed[1] * factor).astype(jnp.bfloat16),
        summed[2] * factor,
        summed[3] * factor,
    )


def solution(mesh):
    return jax.shard_map(
        body,
        mesh=mesh,
        in_specs=(
            P("copy", "space", None, None),
            P("copy", "space", None, None),
            P(None, None, "space", None),
            P(),
            P(),
            P(),
            P(),
        ),
        out_specs=(
            P("copy", "space", None, None),
            P("copy", "space", None, None),
            P(None, None, "space", None),
            P(),
            P(),
            P(),
            P(),
        ),
        check_vma=False,
    )
```

profile of v0, /device:TPU:0, one launch (start us, length us, event | category | flops | bytes accessed | tf_op | source)
XLA Modules:
  0.0 2132.0 jit_solution(13170200237980759754)
XLA Ops:
  7.2 1.0 fusion.93
  8.2 1.0 multiply_convert_fusion.8
  9.2 8.7 copy.67
  17.9 3.8 convert_reduce_fusion
  21.7 4.7 fusion.19
  26.4 0.6 copy-done.23
  27.0 11.1 convert_bitcast_fusion.1
  38.1 31.6 %copy.69 = bf16[2,1,32,256,384]{4,0,2,1,3:T(2,128)(2,1)} copy(bf16[2,1,32,256,384]{3,4,0,2,1:T(8,128)(2,1)} %convert_bitcast_fusion.1) | data formatting | bytes 25165824 | tf_op jit(solution)/shard_map/convert_element_type | solution.py:75
  69.6 7.5 all-to-all-start
  77.2 10.9 fusion.99
  88.1 9.2 copy.125
  97.3 9.1 copy.127
  106.4 1.0 broadcast_multiply_fusion
  107.4 1.1 multiply_convert_fusion.5
  108.6 241.5 %all-to-all-done = bf16[2,1,32,256,384]{4,0,2,1,3:T(2,128)(2,1)} async-done(((bf16[2,1,32,256,384]{4,0,2,1,3:T(2,128)(2,1)}), bf16[2,1,32,256,384]{4,0,2,1,3:T(2,128)(2,1)}, u32[]{:S(2)}, u32[]{:S(2)}) %all-to-all-start) | async-done | bytes 12582944 | tf_op jit(solution)/shard_map/all_to_all | solution.py:76
  350.1 9.5 copy.70
  359.7 6.3 copy.71
  366.0 20.5 fusion.100
  386.5 13.5 fusion.26
  400.0 12.0 fusion.30
  412.0 31.6 %copy.77 = bf16[2,1,256,32,384]{4,0,3,1,2:T(2,128)(2,1)} copy(bf16[2,1,256,32,384]{2,4,0,3,1:T(8,128)(2,1)} %fusion.30) | data formatting | bytes 25165824 | tf_op jit(solution)/shard_map/convert_element_type | solution.py:84
  443.6 276.8 %all_to_all.60 = bf16[2,1,256,32,384]{4,0,3,1,2:T(2,128)(2,1)S(1)} all-to-all(bf16[2,1,256,32,384]{4,0,3,1,2:T(2,128)(2,1)} %copy.77), channel_id=1, replica_groups=mesh['copy'=4,'space'=8] {'space'}, dimensions={2} | all-to-all | bytes 25165824 | tf_op jit(solution)/shard_map/all_to_all | solution.py:85
  720.4 4.8 copy.78
  725.1 6.7 copy.79
  731.8 7.8 bitcast_reduce_fusion
  739.7 2.8 multiply_reduce_fusion.3
  742.4 0.6 copy-done.15
  743.0 2.5 multiply_convert_fusion.2
  745.6 119.2 %multiply_convert_fusion = (bf16[8192,1536]{1,0:T(8,128)(2,1)}, f32[8192,1536]{1,0:T(8,128)}, f32[8192,1536]{1,0:T(8,128)}) fusion(bf16[8192,384]{1,0:T(8,128)(2,1)S(1)} %bitcast.260, bf16[384,1536]{1,0:T(8,128)(2,1)S(1)} %copy-done), kind=kOutput, calls=%fused_computation.3 | convolution fusion | flops 10481565696 | bytes 133300224 | tf_op jit(solution)/shard_map/dot_general | solution.py:98
  864.9 44.2 %add_convert_fusion = bf16[8192,1536]{1,0:T(8,128)(2,1)} fusion(f32[8192,1536]{1,0:T(8,128)} %get-tuple-element.38, f32[8192,1536]{1,0:T(8,128)} %get-tuple-element.55, bf16[8192,384]{1,0:T(8,128)(2,1)} %bitcast.262, bf16[1536,384]{1,0:T(8,128)(2,1)S(1)} %copy-done.30), kind=kOutput, calls=%fused_computation.2 | convolution fusion | flops 9839837184 | bytes 133300224 | tf_op jit(solution)/shard_map/dot_general | solution.py:103
  909.2 20.9 multiply_reduce_fusion.2
  930.1 16.7 multiply_reduce_fusion
  946.9 16.3 convert_bitcast_fusion
  963.2 31.6 %copy.84 = bf16[2,1,32,256,384]{4,0,2,1,3:T(2,128)(2,1)} copy(bf16[2,1,32,256,384]{3,4,0,2,1:T(8,128)(2,1)} %convert_bitcast_fusion) | data formatting | bytes 25165824 | tf_op jit(solution)/shard_map/convert_element_type | solution.py:75
  994.8 277.0 %all_to_all.61 = bf16[2,1,32,256,384]{4,0,2,1,3:T(2,128)(2,1)S(1)} all-to-all(bf16[2,1,32,256,384]{4,0,2,1,3:T(2,128)(2,1)} %copy.84), channel_id=1, replica_groups=mesh['copy'=4,'space'=8] {'space'}, dimensions={3} | all-to-all | bytes 25165824 | tf_op jit(solution)/shard_map/all_to_all | solution.py:76
  1271.8 17.8 copy.85
  1289.6 6.1 copy.86
  1295.8 16.7 copy.87
  1312.5 20.1 fusion.101
  1332.7 13.6 fusion.21
  1346.3 11.5 fusion.32
  1357.8 31.6 %copy.90 = bf16[2,1,256,32,384]{4,0,3,1,2:T(2,128)(2,1)} copy(bf16[2,1,256,32,384]{2,4,0,3,1:T(8,128)(2,1)} %fusion.32) | data formatting | bytes 25165824 | tf_op jit(solution)/shard_map/convert_element_type | solution.py:84
  1389.4 5.3 all-to-all-start.3
  1394.8 18.2 fusion.103
  1413.0 19.7 fusion.104
  1432.8 18.0 fusion.57
  1450.8 17.5 fusion.58
  1468.2 5.3 pad_maximum_fusion
  1473.5 8.7 copy.82
  1482.2 20.9 fusion.102
  1503.1 12.6 copy.81
  1515.7 271.1 %all-reduce.7.cloned.1.call-done = (f32[384,1536]{1,0:T(8,128)}, f32[1536,384]{1,0:T(8,128)}) async-done(((f32[384,1536]{1,0:T(8,128)}, f32[1536,384]{1,0:T(8,128)}), (f32[384,1536]{1,0:T(8,128)}, f32[1536,384]{1,0:T(8,128)})) %all-reduce.7.cloned.1.call-update) | async-done | bytes 4718608 | tf_op jit(solution)/shard_map/psum | solution.py:124
  1786.8 2.9 multiply_convert_fusion.3
  1789.7 2.8 multiply_convert_fusion.4
  1792.5 216.4 %all-reduce.5.cloned.1.call-done = bf16[2,256,32,384]{1,3,2,0:T(8,128)(2,1)} async-done(((bf16[2,256,32,384]{1,3,2,0:T(8,128)(2,1)}), bf16[2,256,32,384]{1,3,2,0:T(8,128)(2,1)}) %all-reduce.5.cloned.1.call-update) | async-done | bytes 12582928 | tf_op jit(solution)/shard_map/psum | solution.py:120
  2008.9 18.2 copy.100
  2027.1 7.7 copy.91
  2034.9 3.3 copy.92
  2038.3 9.4 fusion.18
  2047.7 39.5 %all-reduce = (f32[384]{0:T(512)S(1)}, f32[384]{0:T(512)S(1)}) all-reduce(f32[384]{0:T(512)S(1)} %get-tuple-element.28, f32[384]{0:T(512)S(1)} %copy-done.27), channel_id=1, replica_groups=mesh['copy'=4,'space'=8] {'copy','space'}, use_global_device_ids=true, to_apply=%region_12.13 | all-reduce | flops 768 | bytes 6144 | tf_op jit(solution)/shard_map/psum | solution.py:124
  2087.2 0.6 broadcast_multiply_fusion.7
  2088.4 19.3 fusion.17
  2107.7 8.6 copy.98
  2116.3 8.6 copy.99
  (83 shorter events, 1.0 us)
Async XLA Ops:
  7.2 738.5 %copy-start = (bf16[384,1536]{1,0:T(8,128)(2,1)S(1)}, bf16[384,1536]{1,0:T(8,128)(2,1)}, u32[]{:S(2)}) copy-start(bf16[384,1536]{1,0:T(8,128)(2,1)} %param.10) | copy-start | bytes 3538948
  8.2 723.7 %copy-start.7 = (bf16[1,256,256]{2,1,0:T(8,128)(2,1)}, bf16[1,256,256]{2,1,0:T(8,128)(2,1)S(1)}, u32[]{:S(2)}) copy-start(bf16[1,256,256]{2,1,0:T(8,128)(2,1)S(1)} %fusion.93) | copy-start | bytes 393220
  9.2 722.7 %copy-start.10 = (bf16[1,256,256]{2,1,0:T(8,128)(2,1)}, bf16[1,256,256]{2,1,0:T(8,128)(2,1)S(1)}, u32[]{:S(2)}) copy-start(bf16[1,256,256]{2,1,0:T(8,128)(2,1)S(1)} %multiply_convert_fusion.8) | copy-start | bytes 393220
  9.2 17.8 copy-start.28
  21.6 4.8 copy-start.17
  26.4 0.6 copy-start.23
  69.6 280.5 %all-to-all-start = ((bf16[2,1,32,256,384]{4,0,2,1,3:T(2,128)(2,1)}), bf16[2,1,32,256,384]{4,0,2,1,3:T(2,128)(2,1)}, u32[]{:S(2)}, u32[]{:S(2)}) async-start(bf16[2,1,32,256,384]{4,0,2,1,3:T(2,128)(2,1)} %copy.69), calls=%async_computation | async-start | bytes 25165824 | tf_op jit(solution)/shard_map/all_to_all | solution.py:76
  108.6 257.4 %copy-start.3 = (bf16[1,256,2,256]{3,1,2,0:T(8,128)(2,1)}, bf16[1,256,2,256]{3,1,2,0:T(8,128)(2,1)S(1)}, u32[]{:S(2)}) copy-start(bf16[1,256,2,256]{3,1,2,0:T(8,128)(2,1)S(1)} %get-tuple-element.48) | copy-start | bytes 786436
  108.6 257.4 %copy-start.5 = (bf16[1,256,2,256]{3,1,2,0:T(8,128)(2,1)}, bf16[1,256,2,256]{3,1,2,0:T(8,128)(2,1)S(1)}, u32[]{:S(2)}) copy-start(bf16[1,256,2,256]{3,1,2,0:T(8,128)(2,1)S(1)} %get-tuple-element.51) | copy-start | bytes 786436
  108.6 291.4 %copy-start.19 = (bf16[1,256,2,256]{3,1,2,0:T(8,128)(2,1)}, bf16[1,256,2,256]{3,1,2,0:T(8,128)(2,1)S(1)}, u32[]{:S(2)}) copy-start(bf16[1,256,2,256]{3,1,2,0:T(8,128)(2,1)S(1)} %get-tuple-element.47) | copy-start | bytes 786436
  108.6 291.4 %copy-start.21 = (bf16[1,256,2,256]{3,1,2,0:T(8,128)(2,1)}, bf16[1,256,2,256]{3,1,2,0:T(8,128)(2,1)S(1)}, u32[]{:S(2)}) copy-start(bf16[1,256,2,256]{3,1,2,0:T(8,128)(2,1)S(1)} %get-tuple-element.52) | copy-start | bytes 786436
  739.6 6.0 copy-start.1
  739.6 3.4 copy-start.25
  739.6 6.0 copy-start.13
  742.4 0.6 copy-start.15
  745.6 119.3 %copy-start.2 = (bf16[1,32,256,384]{3,2,1,0:T(8,128)(2,1)}, bf16[1,32,256,384]{3,2,1,0:T(8,128)(2,1)S(1)}, u32[]{:S(2)}) copy-start(bf16[1,32,256,384]{3,2,1,0:T(8,128)(2,1)S(1)} %multiply_convert_fusion.2) | copy-start | bytes 18874372
  745.6 119.3 %copy-start.30 = (bf16[1536,384]{1,0:T(8,128)(2,1)S(1)}, bf16[1536,384]{1,0:T(8,128)(2,1)}, u32[]{:S(2)}) copy-start(bf16[1536,384]{1,0:T(8,128)(2,1)} %param.11) | copy-start | bytes 3538948
  864.9 44.2 %copy-start.26 = (f32[384]{0:T(512)S(1)}, f32[384]{0:T(512)}, u32[]{:S(2)}) copy-start(f32[384]{0:T(512)} %param.13) | copy-start | bytes 4612
  909.1 20.9 copy-start.14
  909.2 20.9 copy-start.16
  930.1 16.8 copy-start.8
  930.1 16.8 copy-start.11
  1295.8 16.7 copy-start.4
  1295.8 16.7 copy-start.6
  1332.6 13.6 copy-start.20
  1332.7 13.6 copy-start.22
  1389.4 637.7 %all-to-all-start.3 = ((bf16[2,1,256,32,384]{4,0,3,1,2:T(2,128)(2,1)}), bf16[2,1,256,32,384]{4,0,3,1,2:T(2,128)(2,1)}, u32[]{:S(2)}, u32[]{:S(2)}) async-start(bf16[2,1,256,32,384]{4,0,3,1,2:T(2,128)(2,1)} %copy.90), calls=%async_computation.3 | async-start | bytes 25165824 | tf_op jit(solution)/shard_map/all_to_all | solution.py:85
  1394.8 392.1 %all-reduce.7.cloned.1.call-start = ((), (), s32[]{:S(2)}) async-start(), calls=%async_computation.5 | async-start | bytes 9437184 | tf_op jit(solution)/shard_map/psum | solution.py:124
  1432.7 576.2 %all-reduce.5.cloned.1.call-start = ((), (), s32[]{:S(2)}) async-start(), calls=%async_computation.4 | async-start | bytes 25165824 | tf_op jit(solution)/shard_map/psum | solution.py:120
  1473.5 8.7 copy-start.31
  2027.1 11.1 slice-start
  2034.8 3.4 slice-start.1
  2034.9 3.4 copy-start.9
  2034.9 3.4 copy-start.12
  2034.9 3.4 copy-start.18
  2034.9 3.4 copy-start.24
  2034.9 3.4 copy-start.29
  2038.3 9.4 copy-start.27
Sparse Core Ops, SparseCore 0:
  1432.8 353.9 all-reduce.6
  1789.4 219.4 all-reduce.4
where the time goes:
time: 2140 us; the launch traced here: 2130 us
  waiting for transfers between devices  729 us (34%)
  blocking collectives  593 us (28%)
  matrix products  352 us (16%)
  local copies, waits for them, and re-layouts  301 us (14%)
  other arithmetic  129 us (6%)
    all_to_all x1, blocking collectives, spectral(): lax.all_to_all(rows, 'space', split_axis=3, concat_axis=2, tiled=True)  277 us
    all_to_all x1, blocking collectives, spectral(): lax.all_to_all(returned, 'space', split_axis=2, concat_axis=3, tiled=True)  277 us
    psum x1, waiting for transfers between devices, body(): lax.psum((local_sums[0], local_sums[1], local_sums[2], local_sums[3]), ('...  271 us
    all_to_all x1, waiting for transfers between devices, spectral(): lax.all_to_all(rows, 'space', split_axis=3, concat_axis=2, tiled=True)  242 us
    psum x1, waiting for transfers between devices, body(): lax.psum(filter_terms.astype(jnp.bfloat16), 'copy').astype(jnp.float32)  216 us
    dot_general x1, matrix products, body(): preact = jnp.dot(mlp_in, weight_in, preferred_element_type=jnp.float32)  119 us
    unnamed x75, local copies, waits for them, and re-layouts  72.4 us
    convert_element_type x2, local copies, waits for them, and re-layouts, spectral(): returned = jnp.einsum('qmph,pbhkc->qbmkc', column_table(height, -1), weig...  63.2 us
  transfers between devices with their start and end apart: 4, of which 3 were waited for; matrix products, arithmetic and copies ran while one was open for 8% of the time, Pallas kernels for 0%

commit v1 on v0

--- a/solution.py
+++ b/solution.py
@@ -1,11 +1,684 @@
+import functools
 import math
 
 import jax
 import jax.numpy as jnp
+import ml_dtypes
+import numpy as np
 from jax import lax
+from jax.experimental import pallas as pl
+from jax.experimental.pallas import tpu as pltpu
 from jax.sharding import PartitionSpec as P
 
 EPS = 1e-06
+LANES = 128
+VMEM_LIMIT = 60 * 1024 * 1024
+BF16 = jnp.bfloat16
+F32 = jnp.float32
+
+
+def dft_pair(length):
+    index = np.arange(length, dtype=np.int64)
+    angle = (index[:, None] * index[None, :] % length) * (2.0 * math.pi / length)
+    factor = 1.0 / math.sqrt(length)
+    rounded = lambda a: a.astype(np.float32).astype(ml_dtypes.bfloat16).astype(np.float32)
+    return rounded(np.cos(angle) * factor), rounded(np.sin(angle) * factor)
+
+
+def row_tables(width, n):
+    cosine, sine = dft_pair(width)
+    own = width // n
+    half = own // 2
+    forward = np.zeros((n, 2, half, width), np.float32)
+    weight = np.full((n, 2, half, 1), 2.0, np.float32)
+    for d in range(n):
+        first = own * d + (1 if d >= n // 2 else 0)
+        forward[d, 0] = cosine[first : first + half]
+        forward[d, 1] = -sine[first : first + half]
+    forward[0, 1, 0] = cosine[width // 2]
+    weight[0, :, 0] = 1.0
+    backward = (forward * weight).reshape(width, width).T
+    return (
+        forward.reshape(width, width).astype(ml_dtypes.bfloat16),
+        np.ascontiguousarray(backward).astype(ml_dtypes.bfloat16),
+    )
+
+
+def column_tables(height, n, chunks):
+    cosine, sine = dft_pair(height)
+    zero = np.zeros_like(cosine)
+    rows = height // n // chunks
+
+    def arrange(blocks):
+        full = np.stack([np.stack(line, axis=1) for line in blocks])
+        full = full.reshape(2 * height, 2, n, chunks, rows)
+        return full.transpose(0, 3, 2, 1, 4).reshape(2 * height, 2 * height)
+
+    middle = arrange([[zero, cosine], [zero, -sine]])
+    first = arrange([[cosine, zero], [-sine, zero]])
+    other = arrange([[cosine, sine], [-sine, cosine]])
+    forward = np.stack([middle, first, other])
+    backward = np.ascontiguousarray(forward.transpose(0, 2, 1))
+    return forward.astype(ml_dtypes.bfloat16), backward.astype(ml_dtypes.bfloat16)
+
+
+def mirror_table(height):
+    table = np.zeros((height, height), np.float32)
+    table[np.arange(height), (-np.arange(height)) % height] = 1.0
+    return table.astype(ml_dtypes.bfloat16)
+
+
+def dot(a, b):
+    return jnp.dot(a, b, preferred_element_type=F32)
+
+
+def dot_tn(a, b):
+    return lax.dot_general(a, b, (((0,), (0,)), ((), ())), preferred_element_type=F32)
+
+
+def normalize(values):
+    centred = values - jnp.mean(values, axis=-1, keepdims=True)
+    variance = jnp.mean(centred * centred, axis=-1, keepdims=True)
+    rstd = lax.rsqrt(variance + EPS)
+    return centred * rstd, rstd
+
+
+def norm_backward(upstream, normed, rstd, gain):
+    scaled = upstream * gain
+    return (
+        scaled
+        - jnp.mean(scaled, axis=-1, keepdims=True)
+        - normed * jnp.mean(scaled * normed, axis=-1, keepdims=True)
+    ) * rstd
+
+
+def gelu_and_slope(v):
+    e = jnp.exp(v * v * -0.5)
+    d = 1.0 + (0.3275911 / math.sqrt(2.0)) * jnp.abs(v)
+    t = pl.reciprocal(d, approx=True)
+    t = t * (2.0 - d * t)
+    poly = 0.5 * 1.061405429
+    for coefficient in (-1.453152027, 1.421413741, -0.284496736, 0.254829592):
+        poly = poly * t + 0.5 * coefficient
+    tail = poly * t * e
+    phi = jnp.where(v < 0.0, tail, 1.0 - tail)
+    return v * phi, phi + v * e * (1.0 / math.sqrt(2.0 * math.pi))
+
+
+def unpack(received, scratch):
+    columns, rows, chans = received.shape
+    for c in range(chans // LANES):
+        part = received[:, :, c * LANES : (c + 1) * LANES].astype(F32)
+        scratch[c] = part.reshape(columns * rows, LANES)
+
+
+def read_row(scratch, row, columns, rows):
+    parts = [
+        scratch[c, pl.ds(row, columns, stride=rows), :].astype(BF16)
+        for c in range(scratch.shape[0])
+    ]
+    return jnp.concatenate(parts, axis=1)
+
+
+def write_row(scratch, row, columns, values):
+    start = pl.multiple_of(row * columns, columns)
+    for c in range(scratch.shape[0]):
+        scratch[c, pl.ds(start, columns), :] = values[:, c * LANES : (c + 1) * LANES]
+
+
+def pack(scratch, outgoing):
+    columns, rows, _ = outgoing.shape
+
+    def step(k, carry):
+        for c in range(scratch.shape[0]):
+            part = scratch[c, pl.ds(k, rows, stride=columns), :]
+            outgoing[k, :, c * LANES : (c + 1) * LANES] = part.astype(BF16)
+        return carry
+
+    lax.fori_loop(0, columns, step, 0, unroll=8)
+
+
+def params():
+    return pltpu.CompilerParams(vmem_limit_bytes=VMEM_LIMIT)
+
+
+def resident(shape):
+    return pl.BlockSpec(shape, lambda *_: (0,) * len(shape), pipeline_mode=pl.Buffered(1))
+
+
+def cost(flops, size):
+    return pl.CostEstimate(flops=int(flops), bytes_accessed=int(size), transcendentals=0)
+
+
+def enter_kernel(tokens, gain, table, outgoing, scratch):
+    step = pl.program_id(0)
+    block, width, _ = tokens.shape
+    for r in range(block):
+        normed, _ = normalize(tokens[r].astype(F32))
+        mixed = (normed * gain[...]).astype(BF16)
+        write_row(scratch, step * block + r, width, dot(table[...], mixed))
+
+    @pl.when(step == pl.num_programs(0) - 1)
+    def _():
+        pack(scratch, outgoing)
+
+
+def enter(tokens, gain, table, chunk, rows, block):
+    _, width, chans = tokens.shape
+    steps = rows // block
+    return pl.pallas_call(
+        enter_kernel,
+        grid=(steps,),
+        in_specs=[
+            pl.BlockSpec((block, width, chans), lambda i: (i + chunk * steps, 0, 0)),
+            resident((1, chans)),
+            resident((width, width)),
+        ],
+        out_specs=resident((width, rows, chans)),
+        out_shape=jax.ShapeDtypeStruct((width, rows, chans), BF16),
+        scratch_shapes=[pltpu.VMEM((chans // LANES, rows * width, LANES), F32)],
+        compiler_params=params(),
+        cost_estimate=cost(2 * rows * width * width * chans, 4 * rows * width * chans),
+        name="enter_rows",
+    )(tokens, gain, table)
+
+
+def mlp_kernel(
+    received, tokens, upstream, gain, table_out, table_in, w_in, w_out, w_in_t, w_out_t, *rest
+):
+    block_out, outgoing, sum_in, sum_out, sum_gain, unpacked, packed = rest[-7:]
+    step = pl.program_id(0)
+    block, width, chans = tokens.shape
+    rows = received.shape[1]
+    hidden = w_in.shape[1]
+    part = min(512, hidden)
+
+    @pl.when(step == 0)
+    def _():
+        unpack(received, unpacked)
+        sum_in[...] = jnp.zeros_like(sum_in)
+        sum_out[...] = jnp.zeros_like(sum_out)
+        sum_gain[...] = jnp.zeros_like(sum_gain)
+
+    spatial = jnp.concatenate(
+        [
+            dot(table_out[...], read_row(unpacked, step * block + r, width, rows))
+            for r in range(block)
+        ],
+        axis=0,
+    )
+    normed, rstd = normalize(spatial)
+    mlp_in = (normed * gain[...]).astype(BF16)
+    grad = upstream[...].reshape(block * width, chans)
+    out = tokens[...].reshape(block * width, chans).astype(F32)
+    grad_mlp = jnp.zeros_like(spatial)
+    for f in range(0, hidden, part):
+        cols = slice(f, f + part)
+        value, slope = gelu_and_slope(dot(mlp_in, w_in[:, cols]))
+        activated = value.astype(BF16)
+        grad_pre = (dot(grad, w_out_t[:, cols]) * slope).astype(BF16)
+        out = out + dot(activated, w_out[cols, :])
+        grad_mlp = grad_mlp + dot(grad_pre, w_in_t[cols, :])
+        sum_out[:, cols] += dot_tn(grad, activated)
+        sum_in[:, cols] += dot_tn(mlp_in, grad_pre)
+    block_out[...] = out.astype(BF16).reshape(block, width, chans)
+    grad_spatial = norm_backward(grad_mlp, normed, rstd, gain[...])
+    sum_gain[0:8] += jnp.sum((grad_mlp * normed).reshape(-1, 8, chans), axis=0)
+    sum_gain[8:16] += jnp.sum((grad_spatial * spatial).reshape(-1, 8, chans), axis=0)
+    sent = grad_spatial.astype(BF16)
+    for r in range(block):
+        values = dot(table_in[...], sent[r * width : (r + 1) * width])
+        write_row(packed, step * block + r, width, values)
+
+    @pl.when(step == pl.num_programs(0) - 1)
+    def _():
+        pack(packed, outgoing)
+
+
+def mlp(received, tokens, upstream, gain, tables, weights, previous, chunk, block):
+    width, rows, chans = received.shape
+    hidden = weights[0].shape[1]
+    steps = rows // block
+    by_rows = pl.BlockSpec((block, width, chans), lambda i: (i + chunk * steps, 0, 0))
+    operands = [received, tokens, upstream, gain, *tables, *weights]
+    in_specs = [
+        resident((width, rows, chans)),
+        by_rows,
+        by_rows,
+        resident((1, chans)),
+        resident((width, width)),
+        resident((width, width)),
+        resident((chans, hidden)),
+        resident((hidden, chans)),
+        resident((hidden, chans)),
+        resident((chans, hidden)),
+    ]
+    aliases = {}
+    if previous is not None:
+        aliases = {len(operands): 0}
+        operands.append(previous)
+        in_specs.append(pl.BlockSpec(memory_space=pl.ANY))
+    flops = 2 * rows * width * chans * (6 * hidden + 2 * width)
+    return pl.pallas_call(
+        mlp_kernel,
+        grid=(steps,),
+        in_specs=in_specs,
+        out_specs=[
+            by_rows,
+            resident((width, rows, chans)),
+            resident((chans, hidden)),
+            resident((chans, hidden)),
+            resident((16, chans)),
+        ],
+        out_shape=[
+            jax.ShapeDtypeStruct(tokens.shape, BF16),
+            jax.ShapeDtypeStruct((width, rows, chans), BF16),
+            jax.ShapeDtypeStruct((chans, hidden), F32),
+            jax.ShapeDtypeStruct((chans, hidden), F32),
+            jax.ShapeDtypeStruct((16, chans), F32),
+        ],
+        scratch_shapes=[
+            pltpu.VMEM((chans // LANES, rows * width, LANES), F32),
+            pltpu.VMEM((chans // LANES, rows * width, LANES), F32),
+        ],
+        input_output_aliases=aliases,
+        compiler_params=params(),
+        cost_estimate=cost(flops, 10 * rows * width * chans),
+        name="mlp_rows",
+    )(*operands)
+
+
+def leave_kernel(received, tokens, upstream, gain, table_out, *rest):
+    grad_tokens, unpacked = rest[-2:]
+    step = pl.program_id(0)
+    block, width, _ = tokens.shape
+    rows = received.shape[1]
+
+    @pl.when(step == 0)
+    def _():
+        unpack(received, unpacked)
+
+    for r in range(block):
+        back = dot(table_out[...], read_row(unpacked, step * block + r, width, rows))
+        normed, rstd = normalize(tokens[r].astype(F32))
+        grad = norm_backward(back, normed, rstd, gain[...])
+        grad_tokens[r] = (upstream[r].astype(F32) + grad).astype(BF16)
+
+
+def leave(received, tokens, upstream, gain, table_out, previous, chunk, block):
+    width, rows, chans = received.shape
+    steps = rows // block
+    by_rows = pl.BlockSpec((block, width, chans), lambda i: (i + chunk * steps, 0, 0))
+    operands = [received, tokens, upstream, gain, table_out]
+    in_specs = [
+        resident((width, rows, chans)),
+        by_rows,
+        by_rows,
+        resident((1, chans)),
+        resident((width, width)),
+    ]
+    aliases = {}
+    if previous is not None:
+        aliases = {len(operands): 0}
+        operands.append(previous)
+        in_specs.append(pl.BlockSpec(memory_space=pl.ANY))
+    return pl.pallas_call(
+        leave_kernel,
+        grid=(steps,),
+        in_specs=in_specs,
+        out_specs=by_rows,
+        out_shape=jax.ShapeDtypeStruct(tokens.shape, BF16),
+        scratch_shapes=[pltpu.VMEM((chans // LANES, rows * width, LANES), F32)],
+        input_output_aliases=aliases,
+        compiler_params=params(),
+        cost_estimate=cost(2 * rows * width * width * chans, 8 * rows * width * chans),
+        name="leave_rows",
+    )(*operands)
+
+
+def transform_in(table, received):
+    parts = [ref[...].reshape(-1, ref.shape[-1]) for ref in received]
+    return dot(table[0], jnp.concatenate(parts, axis=0))
+
+
+def transform_out(table, weighted, outgoing, carried):
+    step = pl.program_id(0)
+    result = dot(table[0], weighted)
+
+    @pl.when(step == 0)
+    def _():
+        carried[...] = result
+
+    result = result + jnp.where(step == 1, carried[...], 0.0)
+    size = result.shape[0] // len(outgoing)
+    for c, ref in enumerate(outgoing):
+        ref[...] = result[c * size : (c + 1) * size].astype(BF16).reshape(ref.shape)
+
+
+def forward_kernel(chunks, flags, table_f, table_b, kernel, *rest):
+    received, outgoing = rest[:chunks], rest[chunks : 2 * chunks]
+    spectrum, carried = rest[2 * chunks :]
+    height = kernel.shape[2]
+    found = transform_in(table_f, received).astype(BF16)
+    spectrum[0] = found.reshape(spectrum.shape[1:])
+    found = found.astype(F32)
+    real, imag = found[:height], found[height:]
+    k_real, k_imag = kernel[0, 0].astype(F32), kernel[0, 1].astype(F32)
+    weighted = jnp.concatenate(
+        [
+            (k_real * real - k_imag * imag).astype(BF16),
+            (k_real * imag + k_imag * real).astype(BF16),
+        ],
+        axis=0,
+    )
+    transform_out(table_b, weighted, outgoing, carried)
+
+
+def backward_kernel(chunks, flags, table_f, table_b, kernel, spectrum, *rest):
+    received, outgoing = rest[:chunks], rest[chunks : 2 * chunks]
+    terms, carried = rest[2 * chunks :]
+    height = kernel.shape[2]
+    found = transform_in(table_f, received).astype(BF16).astype(F32)
+    real, imag = found[:height], found[height:]
+    s_real, s_imag = spectrum[0, 0].astype(F32), spectrum[0, 1].astype(F32)
+    terms[0, 0] = (real * s_real + imag * s_imag).astype(BF16)
+    terms[0, 1] = (imag * s_real - real * s_imag).astype(BF16)
+    k_real, k_imag = kernel[0, 0].astype(F32), kernel[0, 1].astype(F32)
+    weighted = jnp.concatenate(
+        [
+            (k_real * real + k_imag * imag).astype(BF16),
+            (k_real * imag - k_imag * real).astype(BF16),
+        ],
+        axis=0,
+    )
+    transform_out(table_b, weighted, outgoing, carried)
+
+
+def columns(flags, tables, kernel, received, spectrum):
+    chunks = len(received)
+    n, _, half, rows, chans = received[0].shape
+    height = kernel.shape[2]
+    column = pl.BlockSpec(
+        (n, 2, 1, rows, chans), lambda t, flags: (0, 0, jnp.maximum(t - 1, 0), 0, 0)
+    )
+    table = pl.BlockSpec(
+        (1, 2 * height, 2 * height),
+        lambda t, flags: (jnp.where(t == 1, 2 - flags[1], jnp.minimum(t, 1) * 2), 0, 0),
+    )
+    held = pl.BlockSpec((1, 2, height, chans), lambda t, flags: (t, 0, 0, 0))
+    body = forward_kernel if spectrum is None else backward_kernel
+    extra = [] if spectrum is None else [spectrum]
+    return pl.pallas_call(
+        functools.partial(body, chunks),
+        grid_spec=pltpu.PrefetchScalarGridSpec(
+            num_scalar_prefetch=1,
+            grid=(half + 1,),
+            in_specs=[table, table, held] + [held] * len(extra) + [column] * chunks,
+            out_specs=[column] * chunks + [held],
+            scratch_shapes=[pltpu.VMEM((2 * height, chans), F32)],
+        ),
+        out_shape=[jax.ShapeDtypeStruct(r.shape, BF16) for r in received]
+        + [jax.ShapeDtypeStruct(kernel.shape, BF16)],
+        compiler_params=params(),
+        cost_estimate=cost(
+            16 * height * height * chans * (half + 1), 20 * height * chans * (half + 1)
+        ),
+        name="filter_columns",
+    )(flags, *tables, kernel, *extra, *received)
+
+
+def kernel_part_kernel(copies, flags, mirror, own, *rest):
+    mains, extras = rest[:copies], rest[copies : 2 * copies]
+    kernel, scr_own, scr_main, scr_extra = rest[2 * copies :]
+    part = pl.program_id(0)
+    upper, first, me = flags[0], flags[1], flags[2]
+    _, height, wide, lanes = own.shape
+    half = wide // 2
+    share = height // copies
+    scr_own[...] = own[0].astype(F32).reshape(height * wide, lanes)
+    for i in range(copies):
+        owner = jnp.bitwise_xor(me, i)
+        at = pl.multiple_of(owner * (share * half), share * half)
+        scr_main[pl.ds(at, share * half), :] = (
+            mains[i][0].astype(F32).reshape(share * half, lanes)
+        )
+        at = pl.multiple_of(owner * share, share)
+        scr_extra[pl.ds(at, share), :] = extras[i][0].astype(F32)
+    sign = jnp.where(part == 0, 0.5, -0.5)
+    extra = scr_extra[...]
+    middle = 0.5 * extra + sign * dot(mirror[...], extra.astype(BF16))
+    kernel[0, 0] = jnp.where(first == 1, middle, 0.0).astype(BF16)
+    for j in range(half):
+        mine = scr_own[pl.ds(j + upper, height, stride=wide), :]
+        index = half - j - upper
+        if j == 0:
+            other = scr_main[pl.ds(half - 1, height, stride=half), :]
+            lower = jnp.where(first == 1, mine, extra)
+            other = jnp.where(upper == 1, other, lower)
+        else:
+            other = scr_main[pl.ds(index, height, stride=half), :]
+        turned = dot(mirror[...], other.astype(BF16))
+        kernel[j + 1, 0] = (0.5 * mine + sign * turned).astype(BF16)
+
+
+def kernel_part(flags, mirror, own, mains, extras):
+    _, height, wide, chans = own.shape
+    copies = len(mains)
+    half, share = wide // 2, height // copies
+    return pl.pallas_call(
+        functools.partial(kernel_part_kernel, copies),
+        grid_spec=pltpu.PrefetchScalarGridSpec(
+            num_scalar_prefetch=1,
+            grid=(2, chans // LANES),
+            in_specs=[
+                pl.BlockSpec((height, height), lambda p, c, flags: (0, 0)),
+                pl.BlockSpec((1, height, wide, LANES), lambda p, c, flags: (p, 0, 0, c)),
+            ]
+            + [pl.BlockSpec((1, share, half, LANES), lambda p, c, flags: (p, 0, 0, c))] * copies
+            + [pl.BlockSpec((1, share, LANES), lambda p, c, flags: (p, 0, c))] * copies,
+            out_specs=pl.BlockSpec(
+                (half + 1, 1, height, LANES), lambda p, c, flags: (0, p, 0, c)
+            ),
+            scratch_shapes=[
+                pltpu.VMEM((height * wide, LANES), F32),
+                pltpu.VMEM((height * half, LANES), F32),
+                pltpu.VMEM((height, LANES), F32),
+            ],
+        ),
+        out_shape=jax.ShapeDtypeStruct((half + 1, 2, height, chans), BF16),
+        compiler_params=params(),
+        cost_estimate=cost(4 * height * height * chans * half, 16 * height * half * chans),
+        name="filter_part",
+    )(flags, mirror, own, *mains, *extras)
+
+
+def spread_kernel(copies, flags, mirror, *rest):
+    parts, (out, gathered, turned) = rest[:copies], rest[copies:]
+    part = pl.program_id(0)
+    upper, me = flags[0], flags[2]
+    _, height, wide, lanes = out.shape
+    half = wide // 2
+    share = height // copies
+    for i in range(copies):
+        owner = jnp.bitwise_xor(me, i)
+        at = pl.multiple_of(owner * share, share)
+        gathered[:, pl.ds(at, share), :] = parts[i][:, 0]
+    sign = jnp.where(part == 0, 1.0, -1.0)
+    for k in range(wide):
+        if k == 0:
+            index, straight = jnp.where(upper == 1, 2 * half, 0), 1 - upper
+        elif k < half:
+            index, straight = k - upper, 1
+        elif k == half:
+            index, straight = jnp.where(upper == 1, half - 1, 2 * half - 1), upper
+        else:
+            index, straight = half + wide - 1 - k + upper, 0
+        value = gathered[index]
+        if k != 0 and k < half:
+            turned[pl.ds(k * height, height), :] = value.astype(F32)
+        else:
+            other = sign * dot(mirror[...], value)
+            if k == 0 or k == half:
+                other = jnp.where(straight == 1, value.astype(F32), other)
+            turned[pl.ds(k * height, height), :] = other
+
+    def step(m, carry):
+        out[0, m] = turned[pl.ds(m, wide, stride=height), :]
+        return carry
+
+    lax.fori_loop(0, height, step, 0, unroll=8)
+
+
+def spread(flags, mirror, parts, height, wide):
+    slots, _, share, chans = parts[0].shape
+    copies = len(parts)
+    return pl.pallas_call(
+        functools.partial(spread_kernel, copies),
+        grid_spec=pltpu.PrefetchScalarGridSpec(
+            num_scalar_prefetch=1,
+            grid=(2, chans // LANES),
+            in_specs=[pl.BlockSpec((height, height), lambda p, c, flags: (0, 0))]
+            + [pl.BlockSpec((slots, 1, share, LANES), lambda p, c, flags: (0, p, 0, c))] * copies,
+            out_specs=pl.BlockSpec(
+                (1, height, wide, LANES), lambda p, c, flags: (p, 0, 0, c)
+            ),
+            scratch_shapes=[
+                pltpu.VMEM((slots, height, LANES), BF16),
+                pltpu.VMEM((wide * height, LANES), F32),
+            ],
+        ),
+        out_shape=jax.ShapeDtypeStruct((2, height, wide, chans), F32),
+        compiler_params=params(),
+        cost_estimate=cost(2 * height * height * chans * wide, 12 * height * wide * chans),
+        name="filter_gradient",
+    )(flags, mirror, *parts)
+
+
+def swap(value, axis, size, partner):
+    return lax.ppermute(value, axis, [(i, partner(i)) for i in range(size)])
+
+
+def gather_copies(value, copies):
+    parts = {0: value}
+    bit = copies // 2
+    while bit:
+        for key in list(parts):
+            parts[key ^ bit] = swap(parts[key], "copy", copies, lambda i: i ^ bit)
+        bit //= 2
+    return [parts[i] for i in range(copies)]
+
+
+def reduce_copies(value, copies, axis):
+    me = lax.axis_index("copy")
+    bit = 1
+    while bit < copies:
+        size = value.shape[axis] // 2
+        mine = (me // bit) % 2
+        kept = lax.dynamic_slice_in_dim(value, mine * size, size, axis)
+        sent = lax.dynamic_slice_in_dim(value, (1 - mine) * size, size, axis)
+        other = swap(sent, "copy", copies, lambda i: i ^ bit)
+        value = (kept.astype(F32) + other.astype(F32)).astype(value.dtype)
+        bit *= 2
+    return value
+
+
+def share_index(copies):
+    me = lax.axis_index("copy")
+    index = 0 * me
+    bit = 1
+    while bit < copies:
+        index = index * 2 + (me // bit) % 2
+        bit *= 2
+    return index
+
+
+def exchange(value, n):
+    return lax.all_to_all(value, "space", split_axis=0, concat_axis=0, tiled=True)
+
+
+def body(noisy_tokens, grad_out, filter_weight, weight_in, weight_out, gain_one, gain_two):
+    _, rows_dev, width, chans = noisy_tokens.shape
+    height = filter_weight.shape[1]
+    wide = filter_weight.shape[2]
+    half = wide // 2
+    n, copies = lax.axis_size("space"), lax.axis_size("copy")
+    chunks = 2
+    rows = rows_dev // chunks
+    block = 2
+    tokens = noisy_tokens[0]
+    upstream = grad_out[0]
+    me, copy = lax.axis_index("space"), lax.axis_index("copy")
+    table_in, table_out = (jnp.asarray(t) for t in row_tables(width, n))
+    column_tabs = tuple(jnp.asarray(t) for t in column_tables(height, n, chunks))
+    mirror = jnp.asarray(mirror_table(height))
+    gain_a, gain_b = gain_one.reshape(1, chans), gain_two.reshape(1, chans)
+
+    upper = (me >= n // 2).astype(jnp.int32)
+    first = (me == 0).astype(jnp.int32)
+    flags_in = jnp.stack([upper, first, copy.astype(jnp.int32)])
+
+    share = height // copies
+    mine = lax.dynamic_slice_in_dim(filter_weight, copy * share, share, 1)
+    opposite = lambda d: n - 1 - d
+    main = swap(mine[:, :, half:], "space", n, opposite)
+    to_lower = [(n // 2, 0)] + [(e, n - e) for e in range(n // 2 + 1, n)]
+    single = lax.ppermute(mine[:, :, 0], "space", to_lower)
+    mains, singles = gather_copies(main, copies), gather_copies(single, copies)
+
+    split = lambda value: value.reshape(n, 2, half, rows, chans)
+    join = lambda value: value.reshape(width, rows, chans)
+
+    entered = [enter(tokens, gain_a, table_in, c, rows, block) for c in range(chunks)]
+    arrived = [split(exchange(e, n)) for e in entered]
+    kernel = kernel_part(flags_in, mirror, filter_weight, mains, singles)
+    *returned, spectrum = columns(flags_in, column_tabs, kernel, arrived, None)
+
+    weights = (weight_in, weight_out, weight_in.T, weight_out.T)
+    block_out = None
+    sums, entered = [], []
+    for c in range(chunks):
+        received = exchange(join(returned[c]), n)
+        block_out, sent, *local = mlp(
+            received, tokens, upstream, gain_b, (table_out, table_in), weights, block_out, c, block
+        )
+        entered.append(sent)
+        sums.append(local)
+    arrived = [split(exchange(e, n)) for e in entered]
+    sum_in, sum_out, sum_gain = (a + b for a, b in zip(*sums))
+    sum_two = jnp.sum(sum_gain[:8], axis=0)
+    sum_one = jnp.sum(sum_gain[8:], axis=0) / gain_one
+    summed = lax.psum((sum_in, sum_out, sum_one, sum_two), ("copy", "space"))
+
+    *returned, terms = columns(flags_in, column_tabs, kernel, arrived, spectrum)
+    grad_tokens = None
+    for c in range(chunks):
+        received = exchange(join(returned[c]), n)
+        grad_tokens = leave(
+            received, tokens, upstream, gain_a, table_out, grad_tokens, c, block
+        )
+
+    reduced = reduce_copies(terms, copies, 2)
+    mirrored = swap(reduced[1:], "space", n, opposite)
+    to_upper = [(0, n // 2)] + [(d, n - d) for d in range(1, n // 2)]
+    single = lax.ppermute(jnp.where(me == 0, reduced[0], reduced[1]), "space", to_upper)
+    bundle = jnp.concatenate([reduced[1:], mirrored, single[None]], axis=0)
+    flags_out = jnp.stack([upper, first, share_index(copies).astype(jnp.int32)])
+    parts = gather_copies(bundle, copies)
+    order = [int(format(i, "b").zfill(copies.bit_length() - 1)[::-1], 2) for i in range(copies)]
+    parts = [parts[order[i]] for i in range(copies)]
+    grad_filter = spread(flags_out, mirror, parts, height, wide)
+
+    total_tokens = copies * rows_dev * n * width
+    factor = 1.0 / math.sqrt(total_tokens)
+    return (
+        block_out[None],
+        grad_tokens[None],
+        grad_filter,
+        (summed[0] * factor).astype(BF16),
+        (summed[1].T * factor).astype(BF16),
+        summed[2] * factor,
+        summed[3] * factor,
+    )
 
 
 def dft_parts(length):
@@ -31,7 +704,7 @@
     return jnp.stack([upper, lower])
 
 
-def layer_norm(values):
+def plain_layer_norm(values):
     centre = jnp.mean(values, axis=-1, keepdims=True)
     centred = values - centre
     variance = jnp.mean(centred * centred, axis=-1, keepdims=True)
@@ -39,7 +712,7 @@
     return (centred * rstd_value, rstd_value)
 
 
-def norm_backward(upstream, normed, rstd_value, gain):
+def plain_norm_backward(upstream, normed, rstd_value, gain):
     scaled = upstream * gain
     result = (
         scaled
@@ -87,13 +760,13 @@
     return (output, spectrum)
 
 
-def body(noisy_tokens, grad_out, filter_weight, weight_in, weight_out, gain_one, gain_two):
+def plain_body(noisy_tokens, grad_out, filter_weight, weight_in, weight_out, gain_one, gain_two):
     batch, rows_dev, width, chans = noisy_tokens.shape
     inputs = noisy_tokens.astype(jnp.float32)
-    normed_one, rstd_one = layer_norm(inputs)
+    normed_one, rstd_one = plain_layer_norm(inputs)
     mixed_in = (normed_one * gain_one).astype(jnp.bfloat16)
     spatial, spectrum = spectral(mixed_in, filter_weight, 1)
-    normed_two, rstd_two = layer_norm(spatial)
+    normed_two, rstd_two = plain_layer_norm(spatial)
     mlp_in = (normed_two * gain_two).astype(jnp.bfloat16).reshape(-1, chans)
     preact = jnp.dot(mlp_in, weight_in, preferred_element_type=jnp.float32)
     activated = exact_gelu(preact).astype(jnp.bfloat16)
@@ -107,7 +780,7 @@
     grad_mlp = jnp.dot(grad_pre, weight_in.T, preferred_element_type=jnp.float32).reshape(
         inputs.shape
     )
-    grad_spatial, sum_gain_two = norm_backward(grad_mlp, normed_two, rstd_two, gain_two)
+    grad_spatial, sum_gain_two = plain_norm_backward(grad_mlp, normed_two, rstd_two, gain_two)
     back_spatial, adjoint = spectral(grad_spatial.astype(jnp.bfloat16), filter_weight, -1)
     spec_f = spectrum.astype(jnp.float32)
     adj_f = adjoint.astype(jnp.float32)
@@ -118,7 +791,7 @@
         ]
     )
     grad_filter = lax.psum(filter_terms.astype(jnp.bfloat16), "copy").astype(jnp.float32)
-    grad_normed, sum_gain_one = norm_backward(back_spatial, normed_one, rstd_one, gain_one)
+    grad_normed, sum_gain_one = plain_norm_backward(back_spatial, normed_one, rstd_one, gain_one)
     grad_tokens = (grad_out.astype(jnp.float32) + grad_normed).astype(jnp.bfloat16)
     local_sums = (sum_in, sum_out, sum_gain_one, sum_gain_two)
     summed = lax.psum(
@@ -138,8 +811,13 @@
 
 
 def solution(mesh):
+    def program(*arrays):
+        rows_dev, wide = arrays[0].shape[1], arrays[2].shape[2]
+        tiled = rows_dev % 32 == 0 and wide % 16 == 0
+        return (body if tiled else plain_body)(*arrays)
+
     return jax.shard_map(
-        body,
+        program,
         mesh=mesh,
         in_specs=(
             P("copy", "space", None, None),

time: 2140 us -> 1140 us (0.53)
  blocking collectives: 593 us -> 169 us
  matrix products: 352 us -> 0 us
  Pallas kernels: 0 us -> 290 us
  local copies, waits for them, and re-layouts: 301 us -> 33.6 us
  waiting for transfers between devices: 729 us -> 509 us
  other arithmetic: 129 us -> 19.1 us
  starting transfers between devices: 12.9 us -> 92.6 us
    all_to_all x2 -> x1, blocking collectives: 554 us -> 76.9 us  [exchange(): lax.all_to_all(value, 'space', split_axis=0, concat_axis=0, tiled=True)]
    psum x2 -> x1, waiting for transfers between devices: 487 us -> 104 us  [body(): summed = lax.psum((sum_in, sum_out, sum_one, sum_two), ('copy', 'space'))]
    dot_general x14 -> x0, matrix products: 352 us -> none  [the longest x1 119 us: body(): preact = jnp.dot(mlp_in, weight_in, preferred_element_type=jnp.float32)]
    pallas_call x0 -> x10, Pallas kernels: none -> 290 us  [the longest x2 143 us: mlp(): pl.pallas_call(mlp_kernel, grid=(steps,), in_specs=in_specs, out_specs=[b...]
    ppermute x0 -> x15, waiting for transfers between devices: none -> 264 us  [the longest x13 173 us: swap(): return lax.ppermute(value, axis, [(i, partner(i)) for i in range(size)])]
    convert_element_type x4 -> x0, local copies, waits for them, and re-layouts: 126 us -> none  [the longest x2 63.2 us: spectral(): returned = jnp.einsum('qmph,pbhkc->qbmkc', column_table(height, -1), weig...]
    all_to_all x2 -> x7, waiting for transfers between devices: 242 us -> 141 us  [exchange(): lax.all_to_all(value, 'space', split_axis=0, concat_axis=0, tiled=True)]
    all_to_all x2 -> x7, starting transfers between devices: 12.8 us -> 75.5 us  [exchange(): lax.all_to_all(value, 'space', split_axis=0, concat_axis=0, tiled=True)]
  transfers between devices with their start and end apart: 4 -> 23, of which waited for: 3 -> 13; matrix products, arithmetic and copies ran while one was open for 8% -> 4% of each run, Pallas kernels for 0% -> 18%
where the time goes in v1:
time: 1140 us; the launch traced here: 1130 us
  waiting for transfers between devices  509 us (45%)
  Pallas kernels  290 us (25%)
  blocking collectives  169 us (15%)
  starting transfers between devices  92.6 us (8%)
  local copies, waits for them, and re-layouts  33.6 us (3%)
  other arithmetic  19.1 us (2%)
  between operations  14.8 us (1%)
    ppermute x13, waiting for transfers between devices, swap(): return lax.ppermute(value, axis, [(i, partner(i)) for i in range(size)])  173 us
    pallas_call x2, Pallas kernels, mlp(): pl.pallas_call(mlp_kernel, grid=(steps,), in_specs=in_specs, out_specs=[b...  143 us
    all_to_all x7, waiting for transfers between devices, exchange(): lax.all_to_all(value, 'space', split_axis=0, concat_axis=0, tiled=True)  141 us
    psum x1, waiting for transfers between devices, body(): summed = lax.psum((sum_in, sum_out, sum_one, sum_two), ('copy', 'space'))  104 us
    psum x1, blocking collectives, body(): summed = lax.psum((sum_in, sum_out, sum_one, sum_two), ('copy', 'space'))  92 us
    all_to_all x1, blocking collectives, exchange(): lax.all_to_all(value, 'space', split_axis=0, concat_axis=0, tiled=True)  76.9 us
    all_to_all x7, starting transfers between devices, exchange(): lax.all_to_all(value, 'space', split_axis=0, concat_axis=0, tiled=True)  75.5 us
    ppermute x1, waiting for transfers between devices, body(): single = lax.ppermute(mine[:, :, 0], 'space', to_lower)  55.4 us
  transfers between devices with their start and end apart: 23, of which 13 were waited for; matrix products, arithmetic and copies ran while one was open for 4% of the time, Pallas kernels for 18%

profile of v1, /device:TPU:0, one launch (start us, length us, event | category | flops | bytes accessed | tf_op | source)
XLA Modules:
  0.0 1127.6 jit_solution(7182337175746095158)
XLA Ops:
  7.2 1.2 reshape.46.gain
  8.4 12.7 %enter_rows.3 = bf16[256,16,384]{2,1,0:T(8,128)(2,1)} custom-call(bf16[32,256,384]{2,1,0:T(8,128)(2,1)} %bitcast.26, f32[1,384]{1,0:T(1,128)} %reshape.46.gain, bf16[256,256]{1,0:T(8,128)(2,1)} %constant.78.clone.table.table_in), custom_call_target="tpu_custom_call" | custom-call | flops 805306368 | bytes 6291456 | tf_op jit(solution)/shard_map/enter_rows/pallas_call | solution.py:169
  21.1 7.3 all-to-all-start.1
  28.3 12.7 %enter_rows.2 = bf16[256,16,384]{2,1,0:T(8,128)(2,1)} custom-call(bf16[32,256,384]{2,1,0:T(8,128)(2,1)} %bitcast.27, f32[1,384]{1,0:T(1,128)} %reshape.46.gain, bf16[256,256]{1,0:T(8,128)(2,1)} %constant.78.clone.table.table_in), custom_call_target="tpu_custom_call" | custom-call | flops 805306368 | bytes 6291456 | tf_op jit(solution)/shard_map/enter_rows/pallas_call | solution.py:169
  41.0 58.0 %all-to-all-done.1 = bf16[256,16,384]{2,1,0:T(8,128)(2,1)S(1)} async-done(((bf16[256,16,384]{2,1,0:T(8,128)(2,1)}), bf16[256,16,384]{2,1,0:T(8,128)(2,1)S(1)}, u32[]{:S(2)}, u32[]{:S(2)}) %all-to-all-start.1) | async-done | bytes 3145760 | tf_op jit(solution)/shard_map/all_to_all | solution.py:596
  99.1 1.7 copy-done.1
  100.7 4.4 all-to-all-start
  105.2 1.6 constant_dynamic-slice_fusion
  107.2 4.7 collective-permute-start
  111.8 82.2 %collective-permute-done = bf16[2,64,16,384]{3,1,0,2:T(8,128)(2,1)S(1)} collective-permute-done((bf16[2,64,16,384]{3,1,0,2:T(8,128)(2,1)S(1)}, bf16[2,64,16,384]{3,1,0,2:T(8,128)(2,1)S(1)}, u32[]{:S(2)}, u32[]{:S(2)}) %collective-permute-start) | collective-permute-done | bytes 1572896 | tf_op jit(solution)/shard_map/ppermute | solution.py:558
  194.0 1.5 collective-permute-start.2
  195.5 32.9 %collective-permute-done.2 = bf16[2,64,16,384]{3,1,0,2:T(8,128)(2,1)S(1)} collective-permute-done((bf16[2,64,16,384]{3,1,0,2:T(8,128)(2,1)S(1)}, bf16[2,64,16,384]{3,1,0,2:T(8,128)(2,1)S(1)}, u32[]{:S(2)}, u32[]{:S(2)}) %collective-permute-start.2) | collective-permute-done | bytes 1572896 | tf_op jit(solution)/shard_map/ppermute | solution.py:558
  228.4 1.3 constant_dynamic-slice_fusion.3
  229.7 1.3 collective-permute-start.4
  231.0 55.4 %collective-permute-done.4.rest_4_ = bf16[2,64,384]{2,1,0:T(8,128)(2,1)S(1)} collective-permute-done((bf16[2,64,384]{2,1,0:T(8,128)(2,1)S(1)}, bf16[2,64,384]{2,1,0:T(8,128)(2,1)S(1)}, u32[]{:S(2)}, u32[]{:S(2)}) %collective-permute-start.4) | collective-permute-done | bytes 98336 | tf_op jit(solution)/shard_map/ppermute | solution.py:625
  286.5 1.5 collective-permute-start.6
  288.0 3.1 collective-permute-done.6.rest_6_
  291.1 0.7 pad_add_fusion.flags
  291.8 2.1 copy.22.rest_0_
  293.8 2.1 copy.24.rest_2_
  295.9 3.5 copy.23.rest_1_
  299.5 3.5 copy.25.rest_3_
  302.9 0.6 copy-done.8
  303.6 0.6 copy-done.9
  304.2 21.0 %filter_part.1.kernel = bf16[17,2,256,384]{3,2,1,0:T(8,128)(2,1)} custom-call(s32[3]{0:T(128)} %pad_add_fusion.flags, bf16[256,256]{1,0:T(8,128)(2,1)} %constant.82.clone.mirror, bf16[2,256,32,384]{3,2,1,0:T(8,128)(2,1)} %own.1, bf16[2,64,16,384]{3,2,1,0:T(8,128)(2,1)} %copy.22.rest_0_, bf16[2,64,16,384]{3,2,1,0:T(8,128)(2,1)} %copy.23.rest_1_, ...), custom_call_target="tpu_custom_call" | custom-call | flops 1610612736 | bytes 25165824 | tf_op jit(solution)/shard_map/filter_part/pallas_call | solution.py:468
  325.2 23.7 %filter_columns.2 = (bf16[8,2,16,16,384]{4,3,2,1,0:T(8,128)(2,1)}, bf16[8,2,16,16,384]{4,3,2,1,0:T(8,128)(2,1)}, bf16[17,2,256,384]{3,2,1,0:T(8,128)(2,1)}) custom-call(s32[3]{0:T(128)} %pad_add_fusion.flags, bf16[3,512,512]{2,1,0:T(8,128)(2,1)} %constant.80.clone.table_f, bf16[3,512,512]{2,1,0:T(8,128)(2,1)} %constant.81.clone.table_b, ...), custom_call_target="tpu_custom_call" | custom-call | flops 6845104128 | bytes 33423360 | tf_op jit(solution)/shard_map/filter_columns/pallas_call | solution.py:411
  348.9 76.9 %all_to_all.40.received = bf16[256,16,384]{2,1,0:T(8,128)(2,1)} all-to-all(bf16[256,16,384]{2,1,0:T(8,128)(2,1)} %bitcast.42), channel_id=1, replica_groups=mesh['copy'=4,'space'=8] {'space'}, dimensions={0} | all-to-all | bytes 6291456 | tf_op jit(solution)/shard_map/all_to_all | solution.py:596
  425.8 4.0 all-to-all-start.2
  430.4 2.4 copy.26
  432.7 2.4 copy.27
  435.1 71.6 %mlp_rows.2 = (bf16[32,256,384]{2,1,0:T(8,128)(2,1)}, bf16[256,16,384]{2,1,0:T(8,128)(2,1)}, f32[384,1536]{1,0:T(8,128)}, f32[384,1536]{1,0:T(8,128)}, f32[16,384]{1,0:T(8,128)}) custom-call(bf16[256,16,384]{2,1,0:T(8,128)(2,1)} %all_to_all.40.received, bf16[32,256,384]{2,1,0:T(8,128)(2,1)} %bitcast.28, bf16[32,256,384]{2,1,0:T(8,128)(2,1)} %bitcast.32, ...), custom_call_target="tpu_custom_call" | custom-call | flops 30601641984 | bytes 15728640 | tf_op jit(solution)/shard_map/mlp_rows/pallas_call | solution.py:262
  506.7 1.7 copy-done.3
  508.4 6.2 all-to-all-start.4
  514.6 71.6 %mlp_rows.3 = (bf16[32,256,384]{2,1,0:T(8,128)(2,1)}, bf16[256,16,384]{2,1,0:T(8,128)(2,1)}, f32[384,1536]{1,0:T(8,128)}, f32[384,1536]{1,0:T(8,128)}, f32[16,384]{1,0:T(8,128)}) custom-call(bf16[256,16,384]{2,1,0:T(8,128)(2,1)} %copy-done.3, bf16[32,256,384]{2,1,0:T(8,128)(2,1)} %bitcast.29, ...), custom_call_target="tpu_custom_call", output_to_operand_aliasing={{0}: (10, {})} | custom-call | flops 30601641984 | bytes 15728640 | tf_op jit(solution)/shard_map/mlp_rows/pallas_call | solution.py:262
  586.3 1.7 copy-done.2
  588.0 6.0 all-to-all-start.5
  594.0 69.9 %all-to-all-done.5 = bf16[256,16,384]{2,1,0:T(8,128)(2,1)} async-done(((bf16[256,16,384]{2,1,0:T(8,128)(2,1)}), bf16[256,16,384]{2,1,0:T(8,128)(2,1)}, u32[]{:S(2)}, u32[]{:S(2)}) %all-to-all-start.5) | async-done | bytes 3145760 | tf_op jit(solution)/shard_map/all_to_all | solution.py:596
  663.9 25.7 %filter_columns.3 = (bf16[8,2,16,16,384]{4,3,2,1,0:T(8,128)(2,1)}, bf16[8,2,16,16,384]{4,3,2,1,0:T(8,128)(2,1)}, bf16[17,2,256,384]{3,2,1,0:T(8,128)(2,1)}) custom-call(s32[3]{0:T(128)} %pad_add_fusion.flags, bf16[3,512,512]{2,1,0:T(8,128)(2,1)} %constant.80.clone.table_f, bf16[3,512,512]{2,1,0:T(8,128)(2,1)} %constant.81.clone.table_b, ...), custom_call_target="tpu_custom_call" | custom-call | flops 6845104128 | bytes 33423360 | tf_op jit(solution)/shard_map/filter_columns/pallas_call | solution.py:411
  689.6 2.3 constant_dynamic-slice_fusion.2
  692.0 4.5 all-to-all-start.7
  696.5 1.5 collective-permute-done.8
  698.0 4.2 add_convert_fusion
  702.2 1.4 constant_dynamic-slice_fusion.1
  703.7 1.4 collective-permute-start.9
  705.1 37.4 %collective-permute-done.9 = bf16[17,2,64,384]{3,2,1,0:T(8,128)(2,1)} collective-permute-done((bf16[17,2,64,384]{3,2,1,0:T(8,128)(2,1)}, bf16[17,2,64,384]{3,2,1,0:T(8,128)(2,1)}, u32[]{:S(2)}, u32[]{:S(2)}) %collective-permute-start.9) | collective-permute-done | bytes 1671200 | tf_op jit(solution)/shard_map/ppermute | solution.py:558
  742.5 2.0 add_convert_fusion.1
  744.8 3.2 collective-permute-start.10
  748.0 1.8 collective-permute-start.11
  749.8 35.3 %collective-permute-done.11 = bf16[2,64,384]{2,1,0:T(8,128)(2,1)S(1)} collective-permute-done((bf16[2,64,384]{2,1,0:T(8,128)(2,1)S(1)}, bf16[2,64,384]{2,1,0:T(8,128)(2,1)S(1)}, u32[]{:S(2)}, u32[]{:S(2)}) %collective-permute-start.11) | collective-permute-done | bytes 98336 | tf_op jit(solution)/shard_map/ppermute | solution.py:663
  785.1 1.7 collective-permute-done.10
  787.3 1.6 collective-permute-start.12
  788.9 13.3 %all-to-all-done.7.received = bf16[256,16,384]{2,1,0:T(8,128)(2,1)} async-done(((bf16[256,16,384]{2,1,0:T(8,128)(2,1)}), bf16[256,16,384]{2,1,0:T(8,128)(2,1)}, u32[]{:S(2)}, u32[]{:S(2)}) %all-to-all-start.7) | async-done | bytes 3145760 | tf_op jit(solution)/shard_map/all_to_all | solution.py:596
  802.2 43.0 %all-to-all-start.6 = ((bf16[256,16,384]{2,1,0:T(8,128)(2,1)}), bf16[256,16,384]{2,1,0:T(8,128)(2,1)}, u32[]{:S(2)}, u32[]{:S(2)}) async-start(bf16[256,16,384]{2,1,0:T(8,128)(2,1)} %bitcast.37), calls=%async_computation.6 | async-start | bytes 6291456 | tf_op jit(solution)/shard_map/all_to_all | solution.py:596
  845.4 13.9 %collective-permute-done.12.rest_1_ = bf16[33,2,64,384]{3,2,1,0:T(8,128)(2,1)} collective-permute-done((bf16[33,2,64,384]{3,2,1,0:T(8,128)(2,1)S(1)}, bf16[33,2,64,384]{3,2,1,0:T(8,128)(2,1)}, u32[]{:S(2)}, u32[]{:S(2)}) %collective-permute-start.12) | collective-permute-done | bytes 3244064 | tf_op jit(solution)/shard_map/ppermute | solution.py:558
  859.2 4.3 add.63
  863.6 1.8 add.62
  865.4 0.7 pad_add_fusion.2.flags
  866.1 92.0 %all-reduce = (f32[384]{0:T(512)S(1)}, f32[384]{0:T(512)S(1)}) all-reduce(f32[384]{0:T(512)S(1)} %div.17, f32[384]{0:T(512)S(1)} %get-tuple-element.46), channel_id=1, replica_groups=mesh['copy'=4,'space'=8] {'copy','space'}, use_global_device_ids=true, to_apply=%region_3.0 | all-reduce | flops 768 | bytes 6144 | tf_op jit(solution)/shard_map/psum | solution.py:650
  958.8 104.3 %all-reduce.4.cloned.1.call-done = (f32[384,1536]{1,0:T(8,128)}, f32[384,1536]{1,0:T(8,128)}) async-done(((f32[384,1536]{1,0:T(8,128)}, f32[384,1536]{1,0:T(8,128)}), (f32[384,1536]{1,0:T(8,128)}, f32[384,1536]{1,0:T(8,128)})) %all-reduce.4.cloned.1.call-update) | async-done | bytes 4718608 | tf_op jit(solution)/shard_map/psum | solution.py:650
  1063.1 4.3 multiply_convert_fusion.1
  1067.4 2.4 copy.28
  1069.7 12.1 %leave_rows.2.rest_0_ = bf16[32,256,384]{2,1,0:T(8,128)(2,1)} custom-call(bf16[256,16,384]{2,1,0:T(8,128)(2,1)} %all-to-all-done.7.received, bf16[32,256,384]{2,1,0:T(8,128)(2,1)} %bitcast.30, bf16[32,256,384]{2,1,0:T(8,128)(2,1)} %bitcast.34, f32[1,384]{1,0:T(1,128)} %reshape.46.gain, bf16[256,256]{1,0:T(8,128)(2,1)} %constant.79.clone.table_out), custom_call_target="tpu_custom_call" | custom-call | flops 805306368 | bytes 12582912 | tf_op jit(solution)/shard_map/leave_rows/pallas_call | solution.py:325
  1081.9 12.1 %leave_rows.3 = bf16[32,256,384]{2,1,0:T(8,128)(2,1)} custom-call(bf16[256,16,384]{2,1,0:T(8,128)(2,1)} %all-to-all-done.6.received, bf16[32,256,384]{2,1,0:T(8,128)(2,1)} %bitcast.31, bf16[32,256,384]{2,1,0:T(8,128)(2,1)} %bitcast.35, f32[1,384]{1,0:T(1,128)} %reshape.46.gain, ...), custom_call_target="tpu_custom_call", output_to_operand_aliasing={{}: (5, {})} | custom-call | flops 805306368 | bytes 12582912 | tf_op jit(solution)/shard_map/leave_rows/pallas_call | solution.py:325
  1094.0 26.3 %filter_gradient.1 = f32[2,256,32,384]{3,2,1,0:T(8,128)} custom-call(s32[3]{0:T(128)} %pad_add_fusion.2.flags, bf16[256,256]{1,0:T(8,128)(2,1)} %constant.82.clone.mirror, bf16[33,2,64,384]{3,2,1,0:T(8,128)(2,1)} %copy-done, bf16[33,2,64,384]{3,2,1,0:T(8,128)(2,1)} %collective-permute-done.12.rest_1_, ...), custom_call_target="tpu_custom_call" | custom-call | flops 1610612736 | bytes 37748736 | tf_op jit(solution)/shard_map/filter_gradient/pallas_call | solution.py:535
  (52 shorter events, 2.6 us)
Async XLA Ops:
  21.1 78.0 %all-to-all-start.1 = ((bf16[256,16,384]{2,1,0:T(8,128)(2,1)}), bf16[256,16,384]{2,1,0:T(8,128)(2,1)S(1)}, u32[]{:S(2)}, u32[]{:S(2)}) async-start(bf16[256,16,384]{2,1,0:T(8,128)(2,1)} %enter_rows.3), calls=%async_computation.1 | async-start | bytes 6291456 | tf_op jit(solution)/shard_map/all_to_all | solution.py:596
  99.1 1.7 copy-start.1
  100.7 224.5 %all-to-all-start = ((bf16[256,16,384]{2,1,0:T(8,128)(2,1)}), bf16[256,16,384]{2,1,0:T(8,128)(2,1)}, u32[]{:S(2)}, u32[]{:S(2)}) async-start(bf16[256,16,384]{2,1,0:T(8,128)(2,1)} %enter_rows.2), calls=%async_computation | async-start | bytes 6291456 | tf_op jit(solution)/shard_map/all_to_all | solution.py:596
  107.2 86.9 %collective-permute-start = (bf16[2,64,16,384]{3,1,0,2:T(8,128)(2,1)S(1)}, bf16[2,64,16,384]{3,1,0,2:T(8,128)(2,1)S(1)}, u32[]{:S(2)}, u32[]{:S(2)}) collective-permute-start(bf16[2,64,16,384]{3,1,0,2:T(8,128)(2,1)S(1)} %copy.30), channel_id=1, source_target_pairs={{0,7},{1,6},{2,5},{3,4},{4,3},{5,2},{6,1},{7,0},{8,15},{9,14},{10,... | collective-permute-start | bytes 4718600 | tf_op jit(solution)/shard_map/ppermute | solution.py:558
  194.0 34.4 %collective-permute-start.2 = (bf16[2,64,16,384]{3,1,0,2:T(8,128)(2,1)S(1)}, bf16[2,64,16,384]{3,1,0,2:T(8,128)(2,1)S(1)}, u32[]{:S(2)}, u32[]{:S(2)}) collective-permute-start(bf16[2,64,16,384]{3,1,0,2:T(8,128)(2,1)S(1)} %collective-permute-done), channel_id=1, source_target_pairs={{0,16},{8,24},{16,0},{24,8},{1,17},{9,25},{17,1},{25,9},{2,18},{10... | collective-permute-start | bytes 4718600 | tf_op jit(solution)/shard_map/ppermute | solution.py:558
  195.5 100.4 %collective-permute-start.1 = (bf16[2,64,16,384]{3,1,0,2:T(8,128)(2,1)S(1)}, bf16[2,64,16,384]{3,1,0,2:T(8,128)(2,1)}, u32[]{:S(2)}, u32[]{:S(2)}) collective-permute-start(bf16[2,64,16,384]{3,1,0,2:T(8,128)(2,1)S(1)} %collective-permute-done), channel_id=1, source_target_pairs={{0,8},{8,0},{16,24},{24,16},{1,9},{9,1},{17,25},{25,17},{2,10},{10... | collective-permute-start | bytes 4718600 | tf_op jit(solution)/shard_map/ppermute | solution.py:558
  228.4 71.0 %collective-permute-start.3 = (bf16[2,64,16,384]{3,1,0,2:T(8,128)(2,1)S(1)}, bf16[2,64,16,384]{3,1,0,2:T(8,128)(2,1)}, u32[]{:S(2)}, u32[]{:S(2)}) collective-permute-start(bf16[2,64,16,384]{3,1,0,2:T(8,128)(2,1)S(1)} %collective-permute-done.2), channel_id=1, source_target_pairs={{0,8},{8,0},{16,24},{24,16},{1,9},{9,1},{17,25},{25,17},{2,10},{10... | collective-permute-start | bytes 4718600 | tf_op jit(solution)/shard_map/ppermute | solution.py:558
  229.7 56.7 %collective-permute-start.4 = (bf16[2,64,384]{2,1,0:T(8,128)(2,1)S(1)}, bf16[2,64,384]{2,1,0:T(8,128)(2,1)S(1)}, u32[]{:S(2)}, u32[]{:S(2)}) collective-permute-start(bf16[2,64,384]{2,1,0:T(8,128)(2,1)S(1)} %bitcast.47), channel_id=1, source_target_pairs={{4,0},{5,3},{6,2},{7,1},{12,8},{13,11},{14,10},{15,9},{20,16},{21,... | collective-permute-start | bytes 294920 | tf_op jit(solution)/shard_map/ppermute | solution.py:625
  286.5 9.4 copy-start.6
  286.5 4.6 collective-permute-start.6
  288.0 15.0 %collective-permute-start.5 = (bf16[2,64,384]{2,1,0:T(8,128)(2,1)S(1)}, bf16[2,64,384]{2,1,0:T(8,128)(2,1)S(1)}, u32[]{:S(2)}, u32[]{:S(2)}) collective-permute-start(bf16[2,64,384]{2,1,0:T(8,128)(2,1)S(1)} %collective-permute-done.4.rest_4_), channel_id=1, source_target_pairs={{0,8},{8,0},{16,24},{24,16},{1,9},{9,1},{17,25},{25,17},{2,10},{10... | collective-permute-start | bytes 294920 | tf_op jit(solution)/shard_map/ppermute | solution.py:558
  291.1 4.8 copy-start.7
  291.1 11.8 %collective-permute-start.7 = (bf16[2,64,384]{2,1,0:T(8,128)(2,1)S(1)}, bf16[2,64,384]{2,1,0:T(8,128)(2,1)S(1)}, u32[]{:S(2)}, u32[]{:S(2)}) collective-permute-start(bf16[2,64,384]{2,1,0:T(8,128)(2,1)S(1)} %collective-permute-done.6.rest_6_), channel_id=1, source_target_pairs={{0,8},{8,0},{16,24},{24,16},{1,9},{9,1},{17,25},{25,17},{2,10},{10... | collective-permute-start | bytes 294920 | tf_op jit(solution)/shard_map/ppermute | solution.py:558
  302.9 0.6 copy-start.8
  303.6 0.6 copy-start.9
  425.8 4.0 copy-start.13
  425.8 80.9 %all-to-all-start.2 = ((bf16[256,16,384]{2,1,0:T(8,128)(2,1)}), bf16[256,16,384]{2,1,0:T(8,128)(2,1)S(1)}, u32[]{:S(2)}, u32[]{:S(2)}) async-start(bf16[256,16,384]{2,1,0:T(8,128)(2,1)} %bitcast.41), calls=%async_computation.2 | async-start | bytes 6291456 | tf_op jit(solution)/shard_map/all_to_all | solution.py:596
  506.7 1.7 copy-start.3
  508.4 77.9 %all-to-all-start.4 = ((bf16[256,16,384]{2,1,0:T(8,128)(2,1)}), bf16[256,16,384]{2,1,0:T(8,128)(2,1)S(1)}, u32[]{:S(2)}, u32[]{:S(2)}) async-start(bf16[256,16,384]{2,1,0:T(8,128)(2,1)} %get-tuple-element.28), calls=%async_computation.4 | async-start | bytes 6291456 | tf_op jit(solution)/shard_map/all_to_all | solution.py:596
  586.3 1.7 copy-start.2
  588.0 75.9 %all-to-all-start.5 = ((bf16[256,16,384]{2,1,0:T(8,128)(2,1)}), bf16[256,16,384]{2,1,0:T(8,128)(2,1)}, u32[]{:S(2)}, u32[]{:S(2)}) async-start(bf16[256,16,384]{2,1,0:T(8,128)(2,1)} %get-tuple-element.29), calls=%async_computation.5 | async-start | bytes 6291456 | tf_op jit(solution)/shard_map/all_to_all | solution.py:596
  691.9 6.1 collective-permute-start.8
  692.0 110.2 %all-to-all-start.7 = ((bf16[256,16,384]{2,1,0:T(8,128)(2,1)}), bf16[256,16,384]{2,1,0:T(8,128)(2,1)}, u32[]{:S(2)}, u32[]{:S(2)}) async-start(bf16[256,16,384]{2,1,0:T(8,128)(2,1)} %bitcast.38), calls=%async_computation.7 | async-start | bytes 6291456 | tf_op jit(solution)/shard_map/all_to_all | solution.py:596
  703.7 38.9 %collective-permute-start.9 = (bf16[17,2,64,384]{3,2,1,0:T(8,128)(2,1)}, bf16[17,2,64,384]{3,2,1,0:T(8,128)(2,1)}, u32[]{:S(2)}, u32[]{:S(2)}) collective-permute-start(bf16[17,2,64,384]{3,2,1,0:T(8,128)(2,1)} %constant_dynamic-slice_fusion.1), channel_id=1, source_target_pairs={{0,16},{8,24},{16,0},{24,8},{1,17},{9,25},{17,1},{25,9},{2,18},{10... | collective-permute-start | bytes 5013512 | tf_op jit(solution)/shard_map/ppermute | solution.py:558
  744.8 42.0 %collective-permute-start.10 = (bf16[16,2,64,384]{3,2,1,0:T(8,128)(2,1)S(1)}, bf16[16,2,64,384]{3,2,1,0:T(8,128)(2,1)S(1)}, u32[]{:S(2)}, u32[]{:S(2)}) collective-permute-start(bf16[16,2,64,384]{3,2,1,0:T(8,128)(2,1)S(1)} %slice.29), channel_id=1, source_target_pairs={{0,7},{1,6},{2,5},{3,4},{4,3},{5,2},{6,1},{7,0},{8,15},{9,14},{10,... | collective-permute-start | bytes 4718600 | tf_op jit(solution)/shard_map/ppermute | solution.py:558
  748.0 37.1 %collective-permute-start.11 = (bf16[2,64,384]{2,1,0:T(8,128)(2,1)S(1)}, bf16[2,64,384]{2,1,0:T(8,128)(2,1)S(1)}, u32[]{:S(2)}, u32[]{:S(2)}) collective-permute-start(bf16[2,64,384]{2,1,0:T(8,128)(2,1)S(1)} %fusion.1), channel_id=1, source_target_pairs={{0,4},{1,7},{2,6},{3,5},{8,12},{9,15},{10,14},{11,13},{16,20},{17,... | collective-permute-start | bytes 294920 | tf_op jit(solution)/shard_map/ppermute | solution.py:663
  787.3 58.0 %copy-start = (bf16[33,2,64,384]{3,2,1,0:T(8,128)(2,1)}, bf16[33,2,64,384]{3,2,1,0:T(8,128)(2,1)S(1)}, u32[]{:S(2)}) copy-start(bf16[33,2,64,384]{3,2,1,0:T(8,128)(2,1)S(1)} %pad_maximum_fusion.rest_0_) | copy-start | bytes 9732100
  787.3 71.9 %collective-permute-start.12 = (bf16[33,2,64,384]{3,2,1,0:T(8,128)(2,1)S(1)}, bf16[33,2,64,384]{3,2,1,0:T(8,128)(2,1)}, u32[]{:S(2)}, u32[]{:S(2)}) collective-permute-start(bf16[33,2,64,384]{3,2,1,0:T(8,128)(2,1)S(1)} %pad_maximum_fusion.rest_0_), channel_id=1, source_target_pairs={{0,16},{8,24},{16,0},{24,8},{1,17},{9,25},{17,1},{25,9},{2,18},{10... | collective-permute-start | bytes 9732104 | tf_op jit(solution)/shard_map/ppermute | solution.py:558
  802.2 279.7 %all-to-all-start.6 = ((bf16[256,16,384]{2,1,0:T(8,128)(2,1)}), bf16[256,16,384]{2,1,0:T(8,128)(2,1)}, u32[]{:S(2)}, u32[]{:S(2)}) async-start(bf16[256,16,384]{2,1,0:T(8,128)(2,1)} %bitcast.37), calls=%async_computation.6 | async-start | bytes 6291456 | tf_op jit(solution)/shard_map/all_to_all | solution.py:596
  845.2 217.8 %all-reduce.4.cloned.1.call-start = ((), (), s32[]{:S(2)}) async-start(), calls=%async_computation.8 | async-start | bytes 9437184 | tf_op jit(solution)/shard_map/psum | solution.py:650
  845.3 248.7 %collective-permute-start.13 = (bf16[33,2,64,384]{3,2,1,0:T(8,128)(2,1)S(1)}, bf16[33,2,64,384]{3,2,1,0:T(8,128)(2,1)}, u32[]{:S(2)}, u32[]{:S(2)}) collective-permute-start(bf16[33,2,64,384]{3,2,1,0:T(8,128)(2,1)S(1)} %pad_maximum_fusion.rest_0_), channel_id=1, source_target_pairs={{0,8},{8,0},{16,24},{24,16},{1,9},{9,1},{17,25},{25,17},{2,10},{10... | collective-permute-start | bytes 9732104 | tf_op jit(solution)/shard_map/ppermute | solution.py:558
  859.2 234.8 %collective-permute-start.14 = (bf16[33,2,64,384]{3,2,1,0:T(8,128)(2,1)}, bf16[33,2,64,384]{3,2,1,0:T(8,128)(2,1)}, u32[]{:S(2)}, u32[]{:S(2)}) collective-permute-start(bf16[33,2,64,384]{3,2,1,0:T(8,128)(2,1)} %collective-permute-done.12.rest_1_), channel_id=1, source_target_pairs={{0,8},{8,0},{16,24},{24,16},{1,9},{9,1},{17,25},{25,17},{2,10},{10... | collective-permute-start | bytes 9732104 | tf_op jit(solution)/shard_map/ppermute | solution.py:558
  859.2 4.3 copy-start.4
  859.2 4.3 copy-start.5
  865.3 0.7 copy-start.10
  865.3 0.8 copy-start.11
  865.3 0.8 copy-start.12
Sparse Core Ops, SparseCore 0:
  865.5 197.5 all-reduce.3
